TPU v7x, 128 devices: a whole 4x4x4 slice. The times are simulated.
128 devices in a mesh: dp: 4 (over x), ctx: 32 (over z, y, core).
Axes of the slice: x: 4, y: 4, z: 4, core: 2. Of those that a mesh axis runs over, the one named last changes fastest.
Arguments:
- inputs: bfloat16 [16384, 896], P(('dp', 'ctx')), may hold values from -6 to 6
- cotangent: bfloat16 [16384, 896], P(('dp', 'ctx')), may hold values from -6 to 6
- span_order: int32 [64], replicated, may hold values from 0 to 63, as said below
- positions: int32 [16384], P(('dp', 'ctx')), may hold values from 0 to 1023, as said below
- attn_gain: bfloat16 [896], P('dp'), may hold values from 0.5 to 1.5
- qkv_weight: bfloat16 [896, 1152], P('dp'), may hold values from -0.1875 to 0.1875
- qkv_bias: bfloat16 [1152], P('dp'), may hold values from -3 to 3
- out_weight: bfloat16 [896, 896], P('dp'), may hold values from -0.375 to 0.375
- mlp_gain: bfloat16 [896], P('dp'), may hold values from 0.5 to 1.5
- gate_weight: bfloat16 [896, 4864], P('dp'), may hold values from -0.1875 to 0.1875
- up_weight: bfloat16 [896, 4864], P('dp'), may hold values from -0.1875 to 0.1875
- down_weight: bfloat16 [4864, 896], P('dp'), may hold values from -0.078125 to 0.078125
Outputs:
- output: bfloat16 [16384, 896], P(('dp', 'ctx'))
- input_grad: bfloat16 [16384, 896], P(('dp', 'ctx'))
- attn_gain_grad: float32 [896], P('dp')
- qkv_weight_grad: float32 [896, 1152], P('dp')
- qkv_bias_grad: float32 [1024], P('dp')
- value_bias_grad: float32 [128], P('dp')
- out_weight_grad: float32 [896, 896], P('dp')
- mlp_gain_grad: float32 [896], P('dp')
- gate_weight_grad: float32 [896, 4864], P('dp')
- up_weight_grad: float32 [896, 4864], P('dp')
- down_weight_grad: float32 [4864, 896], P('dp')
Inputs may be any that keep to these rules, and one draw needn't show every extreme that they name: `span_order`: entries 2c and 2c + 1 hold two spans j and 63 - j, in either order; every span appears once. `positions`: each token's position within its document. Documents are runs of consecutive places of a sequence, none longer than 1024 tokens, and positions count from 0 at a run's start, increasing by one along place.
All inputs are finite; a program needn't handle non-finite values.
Results may differ from a plain program's by a relative error of at most 0.03.
Values may be sent and summed in bfloat16 or wider, within the bound.
A program may use at most 192 MiB of HBM per device.

v0:
```python
import jax
import jax.numpy as jnp
from jax import lax
from jax.sharding import PartitionSpec as P

QH = 14
KVH = 2
HD = 64
norm_eps = 1e-06
rope_base = 1000000.0
masked_score = -1e30


def rms_apply(values, gain):
    mean_square = jnp.mean(values * values, axis=-1, keepdims=True)
    return values * lax.rsqrt(mean_square + norm_eps) * gain


def half_turn(values):
    middle = values.shape[-1] // 2
    return jnp.concatenate([-values[..., middle:], values[..., :middle]], axis=-1)


def rotate(values, cosine, sine):
    return values * cosine + half_turn(values) * sine


def rope_tables(positions, head_dim):
    middle = head_dim // 2
    inverse = rope_base ** (-(jnp.arange(middle).astype(jnp.float32) * 2.0) / head_dim)
    angles = positions.astype(jnp.float32)[:, None] * inverse[None, :]
    angles = jnp.concatenate([angles, angles], axis=-1)
    return (jnp.cos(angles), jnp.sin(angles))


def span_lookup(table, slots):
    picked = slots[:, None] == jnp.arange(table.shape[0], dtype=jnp.int32)[None, :]
    return jnp.sum(jnp.where(picked, table[None, :], 0), axis=1)


def swiglu(gate_in, up_in):
    return jax.nn.silu(gate_in) * up_in


def body(
    inputs,
    cotangent,
    span_order,
    positions,
    attn_gain,
    qkv_weight,
    qkv_bias,
    out_weight,
    mlp_gain,
    gate_weight,
    up_weight,
    down_weight,
):
    token_count = inputs.shape[0]
    span_rows = token_count // 2
    head_dim = HD
    query_heads = QH
    kv_heads = KVH
    group_size = query_heads // kv_heads
    score_scale = head_dim ** (-0.5)
    q_cols = query_heads * head_dim
    k_cols = kv_heads * head_dim
    seq_length = token_count * lax.axis_size("ctx")
    key_block = min(1024, seq_length)
    block_count = seq_length // key_block
    device_slot = lax.axis_index("ctx")
    local_slots = jnp.arange(token_count, dtype=jnp.int32)
    query_places = (
        span_lookup(span_order, 2 * device_slot + local_slots // span_rows) * span_rows
        + local_slots % span_rows
    )
    all_slots = jnp.arange(seq_length, dtype=jnp.int32)
    key_places = span_lookup(span_order, all_slots // span_rows) * span_rows + all_slots % span_rows
    key_places = key_places.reshape(block_count, key_block)
    gain_one, qkv_full, bias_full, out_full = (
        lax.all_gather(attn_gain, "dp", axis=0, tiled=True),
        lax.all_gather(qkv_weight, "dp", axis=0, tiled=True),
        lax.all_gather(qkv_bias, "dp", axis=0, tiled=True),
        lax.all_gather(out_weight, "dp", axis=0, tiled=True),
    )
    inputs_wide = inputs.astype(jnp.float32)
    gain_one_wide = gain_one.astype(jnp.float32)
    normed_one = rms_apply(inputs_wide, gain_one_wide).astype(jnp.bfloat16)
    mixed_proj = jnp.dot(
        normed_one, qkv_full, preferred_element_type=jnp.float32
    ) + bias_full.astype(jnp.float32)
    cosine, sine = rope_tables(positions, head_dim)
    cosine = cosine[:, None, :]
    sine = sine[:, None, :]
    query_rot = rotate(
        mixed_proj[:, :q_cols].reshape(token_count, query_heads, head_dim), cosine, sine
    ).astype(jnp.bfloat16)
    key_rot = rotate(
        mixed_proj[:, q_cols : q_cols + k_cols].reshape(token_count, kv_heads, head_dim),
        cosine,
        sine,
    )
    key_rot = key_rot.astype(jnp.bfloat16).reshape(token_count, k_cols)
    value_low = mixed_proj[:, q_cols + k_cols :].astype(jnp.bfloat16)
    key_all, value_all = (
        lax.all_gather(key_rot, "ctx", axis=0, tiled=True),
        lax.all_gather(value_low, "ctx", axis=0, tiled=True),
    )
    key_blocks = key_all.reshape(block_count, key_block, kv_heads, head_dim)
    value_blocks = value_all.reshape(block_count, key_block, kv_heads, head_dim)
    query_grouped = query_rot.reshape(token_count, kv_heads, group_size, head_dim)

    def block_scores(key_part, place_part):
        scores = (
            jnp.einsum(
                "qhgd,khd->hgqk", query_grouped, key_part, preferred_element_type=jnp.float32
            )
            * score_scale
        )
        allowed = place_part[None, :] <= query_places[:, None]
        return jnp.where(allowed[None, None], scores, masked_score)

    def max_step(running, pieces):
        running_max, running_sum = running
        scores = block_scores(pieces[0], pieces[1])
        new_max = jnp.maximum(running_max, jnp.max(scores, axis=-1))
        new_sum = running_sum * jnp.exp(running_max - new_max) + jnp.sum(
            jnp.exp(scores - new_max[..., None]), axis=-1
        )
        return ((new_max, new_sum), None)

    start_max = jnp.full((kv_heads, group_size, token_count), masked_score, jnp.float32)
    start_sum = jnp.zeros((kv_heads, group_size, token_count), jnp.float32)
    (final_max, final_sum), unused = lax.scan(
        max_step, (start_max, start_sum), (key_blocks, key_places)
    )
    log_total = final_max + jnp.log(final_sum)

    def value_step(attended_sum, pieces):
        scores = block_scores(pieces[0], pieces[2])
        probs_low = jnp.exp(scores - log_total[..., None]).astype(jnp.bfloat16)
        return (
            attended_sum
            + jnp.einsum(
                "hgqk,khd->qhgd", probs_low, pieces[1], preferred_element_type=jnp.float32
            ),
            None,
        )

    start_total = jnp.zeros((token_count, kv_heads, group_size, head_dim), jnp.float32)
    attended_sum, unused = lax.scan(value_step, start_total, (key_blocks, value_blocks, key_places))
    attended_low = attended_sum.reshape(token_count, q_cols).astype(jnp.bfloat16)
    residual = inputs_wide + jnp.dot(attended_low, out_full, preferred_element_type=jnp.float32)
    gain_two, gate_full, up_full, down_full = (
        lax.all_gather(mlp_gain, "dp", axis=0, tiled=True),
        lax.all_gather(gate_weight, "dp", axis=0, tiled=True),
        lax.all_gather(up_weight, "dp", axis=0, tiled=True),
        lax.all_gather(down_weight, "dp", axis=0, tiled=True),
    )
    gain_two_wide = gain_two.astype(jnp.float32)
    normed_two = rms_apply(residual, gain_two_wide).astype(jnp.bfloat16)
    gate_proj = jnp.dot(normed_two, gate_full, preferred_element_type=jnp.float32)
    up_proj = jnp.dot(normed_two, up_full, preferred_element_type=jnp.float32)
    hidden_low = swiglu(gate_proj, up_proj).astype(jnp.bfloat16)
    output = (residual + jnp.dot(hidden_low, down_full, preferred_element_type=jnp.float32)).astype(
        jnp.bfloat16
    )
    d_hidden = jnp.dot(cotangent, down_full.T, preferred_element_type=jnp.float32)
    down_grad = jnp.dot(hidden_low.T, cotangent, preferred_element_type=jnp.float32)
    swiglu_back = jax.vjp(swiglu, gate_proj, up_proj)[1]
    d_gate, d_up = swiglu_back(d_hidden)
    d_gate = d_gate.astype(jnp.bfloat16)
    d_up = d_up.astype(jnp.bfloat16)
    gate_grad = jnp.dot(normed_two.T, d_gate, preferred_element_type=jnp.float32)
    up_grad = jnp.dot(normed_two.T, d_up, preferred_element_type=jnp.float32)
    d_normed_two = jnp.dot(d_gate, gate_full.T, preferred_element_type=jnp.float32) + jnp.dot(
        d_up, up_full.T, preferred_element_type=jnp.float32
    )
    norm_two_back = jax.vjp(rms_apply, residual, gain_two_wide)[1]
    d_resid_part, gain_two_grad = norm_two_back(d_normed_two)
    d_residual = d_resid_part + cotangent.astype(jnp.float32)
    d_branch = d_residual.astype(jnp.bfloat16)
    out_grad = jnp.dot(attended_low.T, d_branch, preferred_element_type=jnp.float32)
    d_attended = jnp.dot(d_branch, out_full.T, preferred_element_type=jnp.float32).astype(
        jnp.bfloat16
    )
    d_attended = d_attended.reshape(token_count, kv_heads, group_size, head_dim)
    row_delta = jnp.einsum("qhgd,qhgd->hgq", d_attended.astype(jnp.float32), attended_sum)

    def grad_step(d_query, pieces):
        key_part, value_part, place_part = pieces
        scores = block_scores(key_part, place_part)
        probs_full = jnp.exp(scores - log_total[..., None])
        probs_low = probs_full.astype(jnp.bfloat16)
        d_probs = jnp.einsum(
            "qhgd,khd->hgqk", d_attended, value_part, preferred_element_type=jnp.float32
        )
        d_scores = (probs_full * (d_probs - row_delta[..., None])).astype(jnp.bfloat16)
        d_query = (
            d_query
            + jnp.einsum("hgqk,khd->qhgd", d_scores, key_part, preferred_element_type=jnp.float32)
            * score_scale
        )
        d_key = (
            jnp.einsum(
                "hgqk,qhgd->khd", d_scores, query_grouped, preferred_element_type=jnp.float32
            )
            * score_scale
        )
        d_value = jnp.einsum(
            "hgqk,qhgd->khd", probs_low, d_attended, preferred_element_type=jnp.float32
        )
        return (d_query, (d_key, d_value))

    d_query, (d_key_blocks, d_value_blocks) = lax.scan(
        grad_step, start_total, (key_blocks, value_blocks, key_places)
    )
    d_key_all = d_key_blocks.reshape(seq_length, k_cols)
    d_value_all = d_value_blocks.reshape(seq_length, k_cols)
    d_key_own, d_value_own = (
        lax.psum_scatter(
            d_key_all.astype(jnp.bfloat16), "ctx", scatter_dimension=0, tiled=True
        ).astype(jnp.float32),
        lax.psum_scatter(
            d_value_all.astype(jnp.bfloat16), "ctx", scatter_dimension=0, tiled=True
        ).astype(jnp.float32),
    )

    def turn_back(grads):
        return jax.vjp(lambda values: rotate(values, cosine, sine), grads)[1](grads)[0]

    d_query_raw = turn_back(d_query.reshape(token_count, query_heads, head_dim)).reshape(
        token_count, q_cols
    )
    d_key_raw = turn_back(d_key_own.reshape(token_count, kv_heads, head_dim)).reshape(
        token_count, k_cols
    )
    d_mixed = jnp.concatenate([d_query_raw, d_key_raw, d_value_own], axis=1).astype(jnp.bfloat16)
    qkv_grad = jnp.dot(normed_one.T, d_mixed, preferred_element_type=jnp.float32)
    bias_grad = jnp.sum(d_mixed.astype(jnp.float32), axis=0)
    qk_bias_grad = bias_grad[: q_cols + k_cols]
    value_bias_grad = bias_grad[q_cols + k_cols :]
    d_normed_one = jnp.dot(d_mixed, qkv_full.T, preferred_element_type=jnp.float32)
    norm_one_back = jax.vjp(rms_apply, inputs_wide, gain_one_wide)[1]
    d_input_part, gain_one_grad = norm_one_back(d_normed_one)
    input_grad = (d_input_part + d_residual).astype(jnp.bfloat16)
    local_grads = (
        gain_one_grad,
        qkv_grad,
        qk_bias_grad,
        value_bias_grad,
        out_grad,
        gain_two_grad,
        gate_grad,
        up_grad,
        down_grad,
    )
    shard_grads = (
        lax.psum_scatter(
            local_grads[0].astype(jnp.bfloat16), "dp", scatter_dimension=0, tiled=True
        ).astype(jnp.float32),
        lax.psum_scatter(
            local_grads[1].astype(jnp.bfloat16), "dp", scatter_dimension=0, tiled=True
        ).astype(jnp.float32),
        lax.psum_scatter(
            local_grads[2].astype(jnp.bfloat16), "dp", scatter_dimension=0, tiled=True
        ).astype(jnp.float32),
        lax.psum_scatter(
            local_grads[3].astype(jnp.bfloat16), "dp", scatter_dimension=0, tiled=True
        ).astype(jnp.float32),
        lax.psum_scatter(
            local_grads[4].astype(jnp.bfloat16), "dp", scatter_dimension=0, tiled=True
        ).astype(jnp.float32),
        lax.psum_scatter(
            local_grads[5].astype(jnp.bfloat16), "dp", scatter_dimension=0, tiled=True
        ).astype(jnp.float32),
        lax.psum_scatter(
            local_grads[6].astype(jnp.bfloat16), "dp", scatter_dimension=0, tiled=True
        ).astype(jnp.float32),
        lax.psum_scatter(
            local_grads[7].astype(jnp.bfloat16), "dp", scatter_dimension=0, tiled=True
        ).astype(jnp.float32),
        lax.psum_scatter(
            local_grads[8].astype(jnp.bfloat16), "dp", scatter_dimension=0, tiled=True
        ).astype(jnp.float32),
    )
    summed = (
        lax.psum(shard_grads[0].astype(jnp.bfloat16), "ctx").astype(jnp.float32),
        lax.psum(shard_grads[1].astype(jnp.bfloat16), "ctx").astype(jnp.float32),
        lax.psum(shard_grads[2].astype(jnp.bfloat16), "ctx").astype(jnp.float32),
        lax.psum(shard_grads[3].astype(jnp.bfloat16), "ctx").astype(jnp.float32),
        lax.psum(shard_grads[4].astype(jnp.bfloat16), "ctx").astype(jnp.float32),
        lax.psum(shard_grads[5].astype(jnp.bfloat16), "ctx").astype(jnp.float32),
        lax.psum(shard_grads[6].astype(jnp.bfloat16), "ctx").astype(jnp.float32),
        lax.psum(shard_grads[7].astype(jnp.bfloat16), "ctx").astype(jnp.float32),
        lax.psum(shard_grads[8].astype(jnp.bfloat16), "ctx").astype(jnp.float32),
    )
    return (
        output,
        input_grad,
        summed[0],
        summed[1],
        summed[2],
        summed[3],
        summed[4],
        summed[5],
        summed[6],
        summed[7],
        summed[8],
    )


def solution(mesh):
    placed = (
        P(("dp", "ctx"), None),
        P(("dp", "ctx"), None),
        P(),
        P(("dp", "ctx")),
        P("dp"),
        P("dp", None),
        P("dp"),
        P("dp", None),
        P("dp"),
        P("dp", None),
        P("dp", None),
        P("dp", None),
    )
    return jax.shard_map(
        body,
        mesh=mesh,
        in_specs=placed,
        out_specs=(
            P(("dp", "ctx"), None),
            P(("dp", "ctx"), None),
            P("dp"),
            P("dp", None),
            P("dp"),
            P("dp"),
            P("dp", None),
            P("dp"),
            P("dp", None),
            P("dp", None),
            P("dp", None),
        ),
        check_vma=False,
    )
```

profile of v0, /device:TPU:1, one launch (start us, length us, event | category | flops | bytes accessed | tf_op | source)
XLA Modules:
  0.0 1149.0 jit_solution(3470323007845369848)
XLA Ops:
  13.2 9.4 all-reduce.14
  23.7 19.9 %all-gather.8.cloned.1.call-done = bf16[896,1152]{1,0:T(8,128)(2,1)} async-done(((bf16[224,1152]{1,0:T(8,128)(2,1)}), bf16[896,1152]{1,0:T(8,128)(2,1)}) %all-gather.8.cloned.1.call-update) | async-done | bytes 2064400 | tf_op jit(solution)/shard_map/all_gather | solution.py:82
  51.1 38.8 %all-gather.10.cloned.1.call-done = bf16[4096,128]{1,0:T(8,128)(2,1)} async-done(((bf16[128,128]{1,0:T(8,128)(2,1)}), bf16[4096,128]{1,0:T(8,128)(2,1)}) %all-gather.10.cloned.1.call-update) | async-done | bytes 1048592 | tf_op jit(solution)/shard_map/all_gather | solution.py:107
  89.9 5.0 reshape.338
  94.9 5.9 copy.88
  100.7 34.2 %all-gather.12.cloned.1.call-done = bf16[4096,128]{1,0:T(8,128)(2,1)} async-done(((bf16[128,128]{1,0:T(8,128)(2,1)}), bf16[4096,128]{1,0:T(8,128)(2,1)}) %all-gather.12.cloned.1.call-update) | async-done | bytes 1048592 | tf_op jit(solution)/shard_map/all_gather | solution.py:106
  134.9 5.0 reshape.339
  139.9 4.6 copy.89
  144.5 37.0 %while.39 = (s32[]{:T(128)}, f32[2,7,128]{2,1,0:T(8,128)S(1)}, f32[2,7,128]{2,1,0:T(8,128)S(1)}, s32[4,1024]{1,0:T(4,128)S(1)}, s32[128]{0:T(128)S(1)}, /*index=...) while((s32[]{:T(128)}, f32[2,7,128]{2,1,0:T(8,128)S(1)}, ...), condition=%wide.region_6.7_spmd.clone, body=%wide.region_3.6_spmd.clone.sunk | while | flops 247866112 | bytes 15670904 | solution.py:134
  144.8 4.1 fusion.161
  148.9 4.6 exponential_reduce_fusion.2
  153.7 4.1 fusion.161
  157.9 4.6 exponential_reduce_fusion.2
  162.7 4.1 fusion.161
  166.8 4.6 exponential_reduce_fusion.2
  171.7 4.7 fusion.161
  176.3 5.2 exponential_reduce_fusion.2
  181.6 15.2 %while.40 = (s32[]{:T(128)}, f32[128,2,7,64]{0,3,2,1:T(8,128)S(1)}, bf16[4,1024,2,64]{1,3,2,0:T(8,128)(2,1)}, s32[4,1024]{1,0:T(4,128)S(1)}, s32[128]{0:T(128)S(...) while((s32[]{:T(128)}, f32[128,2,7,64]{0,3,2,1:T(8,128)S(1)}, ...), condition=%wide.region_8.9_spmd.clone, body=%wide.region_7.8_spmd.clone.sunk | while | flops 477462528 | bytes 1955962 | solution.py:151
  181.8 3.4 fusion.167
  185.5 3.4 fusion.167
  189.2 3.4 fusion.167
  192.8 3.4 fusion.167
  199.9 49.5 %all-gather.16.cloned.1.call-done = bf16[896,4864]{1,0:T(8,128)(2,1)} async-done(((bf16[224,4864]{1,0:T(8,128)(2,1)}), bf16[896,4864]{1,0:T(8,128)(2,1)}) %all-gather.16.cloned.1.call-update) | async-done | bytes 8716304 | tf_op jit(solution)/shard_map/all_gather | solution.py:156
  249.4 6.4 fusion.102
  255.8 81.9 %all-gather.18.cloned.1.call-done = bf16[896,4864]{1,0:T(8,128)(2,1)} async-done(((bf16[224,4864]{1,0:T(8,128)(2,1)}), bf16[896,4864]{1,0:T(8,128)(2,1)}) %all-gather.18.cloned.1.call-update) | async-done | bytes 8716304 | tf_op jit(solution)/shard_map/all_gather | solution.py:157
  337.7 6.4 fusion.103
  344.1 82.1 %all-gather.20.cloned.1.call-done = bf16[4864,896]{1,0:T(8,128)(2,1)} async-done(((bf16[1216,896]{1,0:T(8,128)(2,1)}), bf16[4864,896]{1,0:T(8,128)(2,1)}) %all-gather.20.cloned.1.call-update) | async-done | bytes 8716304 | tf_op jit(solution)/shard_map/all_gather | solution.py:158
  426.3 7.5 multiply_convert_fusion
  433.8 7.2 fusion.104
  441.1 2.9 multiply_reduce_fusion
  449.2 71.3 %while.41 = (s32[]{:T(128)}, f32[128,2,7,64]{0,3,2,1:T(8,128)S(1)}, bf16[4,1024,2,64]{1,3,2,0:T(8,128)(2,1)}, bf16[4,1024,2,64]{1,3,2,0:T(8,128)(2,1)}, bf16[4,1...) while((s32[]{:T(128)}, f32[128,2,7,64]{0,3,2,1:T(8,128)S(1)}, ...), condition=%wide.region_12.13_spmd.clone, body=%wide.region_11.12_spmd.clone.sunk | while | flops 1193361408 | bytes 99781520 | solution.py:215
  450.8 5.4 fusion.179
  456.2 3.0 fusion.180
  460.9 5.2 fusion.182
  468.6 5.4 fusion.179
  474.0 3.0 fusion.180
  478.7 5.2 fusion.182
  486.4 5.4 fusion.179
  491.8 3.0 fusion.180
  496.5 5.2 fusion.182
  504.1 5.4 fusion.179
  509.6 3.0 fusion.180
  514.3 5.2 fusion.182
  520.5 6.0 copy.124
  526.5 4.7 reshape.332
  531.3 6.0 copy.123
  537.3 4.7 reshape.330
  544.2 64.3 %reduce-scatter.24.cloned.1.call-done = bf16[128,128]{1,0:T(8,128)(2,1)} async-done(((bf16[4096,128]{1,0:T(8,128)(2,1)}), bf16[128,128]{1,0:T(8,128)(2,1)}) %reduce-scatter.24.cloned.1.call-update) | async-done | bytes 32784
  609.3 80.0 %reduce-scatter.22.cloned.1.call-done = bf16[128,128]{1,0:T(8,128)(2,1)} async-done(((bf16[4096,128]{1,0:T(8,128)(2,1)}), bf16[128,128]{1,0:T(8,128)(2,1)}) %reduce-scatter.22.cloned.1.call-update) | async-done | bytes 32784
  692.7 7.2 convolution_convert_fusion.2
  699.9 7.2 convolution_convert_fusion.1
  708.0 4.7 convolution_convert_fusion
  712.9 5.3 reduce-scatter.14.cloned.1.call-done
  718.2 32.8 %reduce-scatter.12.cloned.1.call-done = bf16[224,1152]{1,0:T(8,128)(2,1)} async-done(((bf16[896,1152]{1,0:T(8,128)(2,1)}), bf16[224,1152]{1,0:T(8,128)(2,1)}) %reduce-scatter.12.cloned.1.call-update) | async-done | bytes 516112 | tf_op jit(solution)/shard_map/reduce_scatter | solution.py:262
  751.0 85.4 %reduce-scatter.16.cloned.1.call-done = bf16[224,4864]{1,0:T(8,128)(2,1)} async-done(((bf16[896,4864]{1,0:T(8,128)(2,1)}), bf16[224,4864]{1,0:T(8,128)(2,1)}) %reduce-scatter.16.cloned.1.call-update) | async-done | bytes 2179088 | tf_op jit(solution)/shard_map/reduce_scatter | solution.py:277
  836.4 85.4 %reduce-scatter.18.cloned.1.call-done = bf16[224,4864]{1,0:T(8,128)(2,1)} async-done(((bf16[896,4864]{1,0:T(8,128)(2,1)}), bf16[224,4864]{1,0:T(8,128)(2,1)}) %reduce-scatter.18.cloned.1.call-update) | async-done | bytes 2179088 | tf_op jit(solution)/shard_map/reduce_scatter | solution.py:280
  921.7 85.4 %reduce-scatter.20.cloned.1.call-done = bf16[1216,896]{1,0:T(8,128)(2,1)} async-done(((bf16[4864,896]{1,0:T(8,128)(2,1)}), bf16[1216,896]{1,0:T(8,128)(2,1)}) %reduce-scatter.20.cloned.1.call-update) | async-done | bytes 2179088 | tf_op jit(solution)/shard_map/reduce_scatter | solution.py:283
  1009.2 5.8 fusion.65
  1016.0 7.1 all-reduce.13
  1023.4 65.2 %all-reduce.11 = (bf16[224]{0:T(256)(128)(2,1)S(1)}, bf16[256]{0:T(256)(128)(2,1)S(1)}, bf16[32]{0:T(256)(128)(2,1)S(1)}, bf16[224]{0:T(256)(128)(2,1)S(1)}) all-reduce(bf16[224]{0:T(256)(128)(2,1)S(1)} %dynamic-slice.4, bf16[256]{0:T(256)(128)(2,1)S(1)} %dynamic-slice.6, ...), channel_id=1, replica_groups=mesh['dp'=4,'ctx'=32] {'ctx'}, use_global_device_ids=true, to_apply=%region_18.19 | all-reduce | flops 736 | bytes 2944 | tf_op jit(solution)/shard_map/psum | solution.py:288
  1091.7 39.1 %all-reduce.17.cloned.1.call-done = (bf16[224,1152]{1,0:T(8,128)(2,1)}, bf16[224,896]{1,0:T(8,128)(2,1)}, bf16[224,4864]{1,0:T(8,128)(2,1)}, bf16[224,4864]{1,0:T(8,128)(2,1)}, bf16[1216,896]{1,0:T(8,128)(2,1)}) async-done(((bf16[224,1152]{1,0:T(8,128)(2,1)}, bf16[224,896]{1,0:T(8,128)(2,1)}, bf16[224,4864]{1,0:T(8,128)(2,1)}, bf16[224,4864]{1,0:T(8,128)(2,1)}, bf16[1216,896]{1,0:T(8,128)(2,1)}), ...) | async-done | bytes 7454736 | tf_op jit(solution)/shard_map/psum | solution.py:289
  1135.1 2.3 convert_element_type.199
  1137.5 2.3 convert_element_type.201
  1139.9 2.3 convert_element_type.203
  (267 shorter events, 55.6 us)
Async XLA Ops:
  7.2 39.3 %copy-start.31 = (s32[128]{0:T(128)S(1)}, s32[128]{0:T(128)}, u32[]{:S(2)}) copy-start(s32[128]{0:T(128)} %param.21) | copy-start | bytes 1540
  7.2 36.4 %all-gather.8.cloned.1.call-start = ((), (), s32[]{:S(2)}) async-start(), calls=%async_computation.7 | async-start | bytes 2580480 | tf_op jit(solution)/shard_map/all_gather | solution.py:82
  7.9 82.0 %all-gather.10.cloned.1.call-start = ((), (), s32[]{:S(2)}) async-start(), calls=%async_computation.8 | async-start | bytes 1081344 | tf_op jit(solution)/shard_map/all_gather | solution.py:107
  23.7 23.3 %copy-start.29 = (f32[128]{0:T(128)}, f32[128]{0:T(128)S(1)}, u32[]{:S(2)}) copy-start(f32[128]{0:T(128)S(1)} %fusion.73) | copy-start | bytes 1540
  46.5 88.4 %all-gather.12.cloned.1.call-start = ((), (), s32[]{:S(2)}) async-start(), calls=%async_computation.9 | async-start | bytes 1081344 | tf_op jit(solution)/shard_map/all_gather | solution.py:106
  47.0 3.4 copy-start.28
  47.7 149.1 %all-gather.14.cloned.1.call-start = ((), (), s32[]{:S(2)}) async-start(), calls=%async_computation.10 | async-start | bytes 2007040 | tf_op jit(solution)/shard_map/all_gather | solution.py:84
  48.3 201.1 %all-gather.16.cloned.1.call-start = ((), (), s32[]{:S(2)}) async-start(), calls=%async_computation.11 | async-start | bytes 10895360 | tf_op jit(solution)/shard_map/all_gather | solution.py:156
  48.9 288.8 %all-gather.18.cloned.1.call-start = ((), (), s32[]{:S(2)}) async-start(), calls=%async_computation.12 | async-start | bytes 10895360 | tf_op jit(solution)/shard_map/all_gather | solution.py:157
  49.5 376.8 %all-gather.20.cloned.1.call-start = ((), (), s32[]{:S(2)}) async-start(), calls=%async_computation.13 | async-start | bytes 10895360 | tf_op jit(solution)/shard_map/all_gather | solution.py:158
  50.2 558.2 %reduce-scatter.24.cloned.1.call-start = ((), (), s32[]{:S(2)}) async-start(), calls=%async_computation.20 | async-start | bytes 1081344
  181.5 15.3 %copy-start.9 = (bf16[128,896]{1,0:T(8,128)(2,1)S(1)}, bf16[128,896]{1,0:T(8,128)(2,1)}, u32[]{:S(2)}) copy-start(bf16[128,896]{1,0:T(8,128)(2,1)} %param.18) | copy-start | bytes 688132
  196.7 59.0 %copy-start.19 = (f32[128,2,7,64]{0,3,2,1:T(8,128)}, f32[128,2,7,64]{0,3,2,1:T(8,128)S(1)}, u32[]{:S(2)}) copy-start(f32[128,2,7,64]{0,3,2,1:T(8,128)S(1)} %get-tuple-element.157) | copy-start | bytes 1376260
  196.8 59.0 %copy-start.17 = (bf16[128,2,7,64]{0,3,2,1:T(8,128)(2,1)}, bf16[128,2,7,64]{0,3,2,1:T(8,128)(2,1)S(1)}, u32[]{:S(2)}) copy-start(bf16[128,2,7,64]{0,3,2,1:T(8,128)(2,1)S(1)} %convert_element_type.171) | copy-start | bytes 688132
  433.8 7.2 copy-start.12
  433.8 7.2 copy-start.11
  433.8 7.2 copy-start.2
  433.8 7.2 copy-start.4
  441.1 2.9 copy-start.24
  441.1 3.9 copy-start.8
  449.4 1.4 copy-start.26
  450.5 5.7 copy-start.1
  456.2 3.1 copy-start
  456.2 3.4 copy-start.20
  456.2 4.7 copy-start.22
  456.2 4.7 copy-start.27
  460.9 5.3 copy-start.21
  467.2 1.4 copy-start.26
  468.3 5.7 copy-start.1
  474.0 3.1 copy-start
  474.0 3.4 copy-start.20
  474.0 4.7 copy-start.22
  474.0 4.7 copy-start.27
  478.7 5.3 copy-start.21
  484.9 1.4 copy-start.26
  486.1 5.7 copy-start.1
  491.8 3.1 copy-start
  491.8 3.4 copy-start.20
  491.8 4.7 copy-start.22
  491.8 4.7 copy-start.27
  496.4 5.3 copy-start.21
  502.7 1.4 copy-start.26
  503.9 5.7 copy-start.1
  509.6 3.1 copy-start
  509.6 3.4 copy-start.20
  509.6 4.7 copy-start.22
  509.6 4.7 copy-start.27
  514.2 5.3 copy-start.21
  531.2 158.1 %reduce-scatter.22.cloned.1.call-start = ((), (), s32[]{:S(2)}) async-start(), calls=%async_computation.19 | async-start | bytes 1081344
  531.3 10.9 copy-start.7
  531.3 10.9 copy-start.18
  542.1 148.1 %copy-start.10 = (bf16[128,896]{1,0:T(8,128)(2,1)S(1)}, bf16[128,896]{1,0:T(8,128)(2,1)}, u32[]{:S(2)}) copy-start(bf16[128,896]{1,0:T(8,128)(2,1)} %param.18) | copy-start | bytes 688132
  542.1 176.0 %reduce-scatter.14.cloned.1.call-start = ((), (), s32[]{:S(2)}) async-start(), calls=%async_computation.15 | async-start | bytes 2007040 | tf_op jit(solution)/shard_map/reduce_scatter | solution.py:271
  543.9 207.0 %reduce-scatter.12.cloned.1.call-start = ((), (), s32[]{:S(2)}) async-start(), calls=%async_computation.14 | async-start | bytes 2580480 | tf_op jit(solution)/shard_map/reduce_scatter | solution.py:262
  692.4 144.0 %reduce-scatter.16.cloned.1.call-start = ((), (), s32[]{:S(2)}) async-start(), calls=%async_computation.16 | async-start | bytes 10895360 | tf_op jit(solution)/shard_map/reduce_scatter | solution.py:277
  699.8 221.9 %reduce-scatter.18.cloned.1.call-start = ((), (), s32[]{:S(2)}) async-start(), calls=%async_computation.17 | async-start | bytes 10895360 | tf_op jit(solution)/shard_map/reduce_scatter | solution.py:280
  707.1 300.0 %reduce-scatter.20.cloned.1.call-start = ((), (), s32[]{:S(2)}) async-start(), calls=%async_computation.18 | async-start | bytes 10895360 | tf_op jit(solution)/shard_map/reduce_scatter | solution.py:283
  712.8 418.0 %all-reduce.17.cloned.1.call-start = ((), (), s32[]{:S(2)}) async-start(), calls=%async_computation.21 | async-start | bytes 14909440 | tf_op jit(solution)/shard_map/psum | solution.py:289
  1007.1 2.0 copy-start.5
  1009.1 6.0 copy-start.16
  1014.9 75.9 %copy-start.30 = (f32[128]{0:T(128)S(1)}, f32[128]{0:T(128)}, u32[]{:S(2)}) copy-start(f32[128]{0:T(128)} %copy-done.29) | copy-start | bytes 1540
  1130.8 4.3 copy-start.15
  1133.0 4.4 copy-start.14
  1137.5 2.5 copy-start.13
  (7 other events, 6.5 us)
Sparse Core Ops, SparseCore 0:
  9.7 33.8 all-gather.7
  46.6 43.2 all-gather.9
  92.8 42.0 all-gather.11
  136.4 25.5 all-gather.13
  163.5 85.8 all-gather.15
  250.9 86.7 all-gather.17
  339.4 86.8 all-gather.19
  531.4 77.0 reduce-scatter.23
  612.4 76.9 reduce-scatter.21
  692.2 25.9 reduce-scatter.13
  721.2 29.7 reduce-scatter.11
  753.5 82.8 reduce-scatter.15
  838.8 82.8 reduce-scatter.17
  924.2 82.8 reduce-scatter.19
  1011.1 119.6 all-reduce.16
where the time goes:
time: 1160 us; the launch traced here: 1150 us
  waiting for transfers between devices  787 us (68%)
  matrix products  160 us (14%)
  blocking collectives  81.7 us (7%)
  local copies, waits for them, and re-layouts  59.3 us (5%)
  other arithmetic  40.1 us (3%)
  between operations  18.1 us (2%)
    unnamed x17, waiting for transfers between devices  147 us
    reduce_scatter x1, waiting for transfers between devices, body(): lax.psum_scatter(local_grads[6].astype(jnp.bfloat16), 'dp', scatter_dimen...  85.4 us
    reduce_scatter x1, waiting for transfers between devices, body(): lax.psum_scatter(local_grads[8].astype(jnp.bfloat16), 'dp', scatter_dimen...  85.4 us
    reduce_scatter x1, waiting for transfers between devices, body(): lax.psum_scatter(local_grads[7].astype(jnp.bfloat16), 'dp', scatter_dimen...  85.4 us
    all_gather x1, waiting for transfers between devices, body(): lax.all_gather(down_weight, 'dp', axis=0, tiled=True)  82.1 us
    all_gather x1, waiting for transfers between devices, body(): lax.all_gather(up_weight, 'dp', axis=0, tiled=True)  81.9 us
    psum x1, blocking collectives, body(): lax.psum(shard_grads[0].astype(jnp.bfloat16), 'ctx').astype(jnp.float32)  65.2 us
    all_gather x1, waiting for transfers between devices, body(): lax.all_gather(gate_weight, 'dp', axis=0, tiled=True)  49.5 us
  transfers between devices with their start and end apart: 15, of which 14 were waited for; matrix products, arithmetic and copies ran while one was open for 12% of the time, Pallas kernels for 0%

commit v1 on v0

--- a/solution.py
+++ b/solution.py
@@ -103,7 +103,9 @@
     key_rot = key_rot.astype(jnp.bfloat16).reshape(token_count, k_cols)
     value_low = mixed_proj[:, q_cols + k_cols :].astype(jnp.bfloat16)
     key_all, value_all = (
-        lax.all_gather(key_rot, "ctx", axis=0, tiled=True),
+        jnp.concatenate(
+            lax.all_to_all(jnp.stack([key_rot] * lax.axis_size("ctx")), "ctx", 0, 0), axis=0
+        ),
         lax.all_gather(value_low, "ctx", axis=0, tiled=True),
     )
     key_blocks = key_all.reshape(block_count, key_block, kv_heads, head_dim)

time: 1160 us -> 1120 us (0.966)
  waiting for transfers between devices: 787 us -> 746 us
    all_gather x1, waiting for transfers between devices: 38.8 us -> 0.02 us  [body(): lax.all_gather(value_low, 'ctx', axis=0, tiled=True)]
    all_gather x1 -> x0, waiting for transfers between devices: 34.2 us -> none  [body(): lax.all_gather(key_rot, 'ctx', axis=0, tiled=True)]
    all_to_all x0 -> x1, waiting for transfers between devices: none -> 17 us  [body(): lax.all_to_all(jnp.stack([key_rot] * lax.axis_size('ctx')), 'ctx', 0, 0)]
    all_gather x1, waiting for transfers between devices: 49.5 us -> 64.4 us  [body(): lax.all_gather(gate_weight, 'dp', axis=0, tiled=True)]
    unnamed x17 -> x16, waiting for transfers between devices: 147 us -> 147 us
  transfers between devices with their start and end apart: 15 -> 15, of which waited for: 14 -> 13; matrix products, arithmetic and copies ran while one was open for 12% -> 12% of each run, Pallas kernels for 0% -> 0%
where the time goes in v1:
time: 1120 us; the launch traced here: 1110 us
  waiting for transfers between devices  746 us (67%)
  matrix products  160 us (14%)
  blocking collectives  81.6 us (7%)
  local copies, waits for them, and re-layouts  54.4 us (5%)
  other arithmetic  39.2 us (4%)
  between operations  18.2 us (2%)
    unnamed x16, waiting for transfers between devices  147 us
    reduce_scatter x1, waiting for transfers between devices, body(): lax.psum_scatter(local_grads[6].astype(jnp.bfloat16), 'dp', scatter_dimen...  85.5 us
    reduce_scatter x1, waiting for transfers between devices, body(): lax.psum_scatter(local_grads[8].astype(jnp.bfloat16), 'dp', scatter_dimen...  85.5 us
    reduce_scatter x1, waiting for transfers between devices, body(): lax.psum_scatter(local_grads[7].astype(jnp.bfloat16), 'dp', scatter_dimen...  85.2 us
    all_gather x1, waiting for transfers between devices, body(): lax.all_gather(down_weight, 'dp', axis=0, tiled=True)  82 us
    all_gather x1, waiting for transfers between devices, body(): lax.all_gather(up_weight, 'dp', axis=0, tiled=True)  82 us
    psum x1, blocking collectives, body(): lax.psum(shard_grads[0].astype(jnp.bfloat16), 'ctx').astype(jnp.float32)  65.2 us
    all_gather x1, waiting for transfers between devices, body(): lax.all_gather(gate_weight, 'dp', axis=0, tiled=True)  64.4 us
  transfers between devices with their start and end apart: 15, of which 13 were waited for; matrix products, arithmetic and copies ran while one was open for 12% of the time, Pallas kernels for 0%

profile of v1, /device:TPU:1, one launch (start us, length us, event | category | flops | bytes accessed | tf_op | source)
XLA Modules:
  0.0 1109.0 jit_solution(2735556663232730251)
XLA Ops:
  13.2 9.4 all-reduce.14
  23.7 19.9 %all-gather.7.cloned.1.call-done = bf16[896,1152]{1,0:T(8,128)(2,1)} async-done(((bf16[224,1152]{1,0:T(8,128)(2,1)}), bf16[896,1152]{1,0:T(8,128)(2,1)}) %all-gather.7.cloned.1.call-update) | async-done | bytes 2064400 | tf_op jit(solution)/shard_map/all_gather | solution.py:82
  43.5 2.3 convolution_add_fusion
  51.2 7.6 all-to-all-start
  59.4 17.0 %all-to-all-done = bf16[32,128,128]{1,2,0:T(8,128)(2,1)S(1)} async-done(((bf16[32,128,128]{1,2,0:T(8,128)(2,1)}), bf16[32,128,128]{1,2,0:T(8,128)(2,1)S(1)}, u32[]{:S(2)}, u32[]{:S(2)}) %all-to-all-start) | async-done | bytes 1048608 | tf_op jit(solution)/shard_map/all_to_all | solution.py:107
  79.7 36.1 %while.39 = (s32[]{:T(128)}, f32[2,7,128]{2,1,0:T(8,128)S(1)}, f32[2,7,128]{2,1,0:T(8,128)S(1)}, s32[4,1024]{1,0:T(4,128)S(1)}, s32[128]{0:T(128)S(1)}, /*index=...) while((s32[]{:T(128)}, f32[2,7,128]{2,1,0:T(8,128)S(1)}, ...), condition=%wide.region_6.7_spmd.clone, body=%wide.region_3.6_spmd.clone.sunk | while | flops 247866112 | bytes 15670904 | solution.py:136
  80.0 4.1 fusion.161
  84.1 4.7 exponential_reduce_fusion.2
  89.0 4.1 fusion.161
  93.1 4.6 exponential_reduce_fusion.2
  98.0 4.1 fusion.161
  102.1 4.7 exponential_reduce_fusion.2
  107.1 4.1 fusion.161
  111.2 4.6 exponential_reduce_fusion.2
  115.9 5.0 reshape.338
  120.9 5.9 copy.89
  126.8 15.2 %while.40 = (s32[]{:T(128)}, f32[128,2,7,64]{0,3,2,1:T(8,128)S(1)}, bf16[4,1024,2,64]{1,3,2,0:T(8,128)(2,1)}, s32[4,1024]{1,0:T(4,128)S(1)}, s32[128]{0:T(128)S(...) while((s32[]{:T(128)}, f32[128,2,7,64]{0,3,2,1:T(8,128)S(1)}, ...), condition=%wide.region_8.9_spmd.clone, body=%wide.region_7.8_spmd.clone.sunk | while | flops 477462528 | bytes 1955962 | solution.py:153
  127.0 3.4 fusion.167
  130.7 3.4 fusion.167
  134.4 3.5 fusion.167
  138.1 3.4 fusion.167
  145.1 64.4 %all-gather.13.cloned.1.call-done = bf16[896,4864]{1,0:T(8,128)(2,1)} async-done(((bf16[224,4864]{1,0:T(8,128)(2,1)}), bf16[896,4864]{1,0:T(8,128)(2,1)}) %all-gather.13.cloned.1.call-update) | async-done | bytes 8716304 | tf_op jit(solution)/shard_map/all_gather | solution.py:158
  209.5 6.4 fusion.102
  215.9 82.0 %all-gather.15.cloned.1.call-done = bf16[896,4864]{1,0:T(8,128)(2,1)} async-done(((bf16[224,4864]{1,0:T(8,128)(2,1)}), bf16[896,4864]{1,0:T(8,128)(2,1)}) %all-gather.15.cloned.1.call-update) | async-done | bytes 8716304 | tf_op jit(solution)/shard_map/all_gather | solution.py:159
  297.9 6.4 fusion.103
  304.3 82.0 %all-gather.17.cloned.1.call-done = bf16[4864,896]{1,0:T(8,128)(2,1)} async-done(((bf16[1216,896]{1,0:T(8,128)(2,1)}), bf16[4864,896]{1,0:T(8,128)(2,1)}) %all-gather.17.cloned.1.call-update) | async-done | bytes 8716304 | tf_op jit(solution)/shard_map/all_gather | solution.py:160
  386.3 7.5 multiply_convert_fusion
  393.8 7.2 fusion.104
  401.1 2.9 multiply_reduce_fusion
  409.2 71.4 %while.41 = (s32[]{:T(128)}, f32[128,2,7,64]{0,3,2,1:T(8,128)S(1)}, bf16[4,1024,2,64]{1,3,2,0:T(8,128)(2,1)}, bf16[4,1024,2,64]{1,3,2,0:T(8,128)(2,1)}, bf16[4,1...) while((s32[]{:T(128)}, f32[128,2,7,64]{0,3,2,1:T(8,128)S(1)}, ...), condition=%wide.region_12.13_spmd.clone, body=%wide.region_11.12_spmd.clone.sunk | while | flops 1193361408 | bytes 99781520 | solution.py:217
  410.8 5.4 fusion.179
  416.2 3.0 fusion.180
  420.9 5.2 fusion.182
  428.6 5.4 fusion.179
  434.0 3.0 fusion.180
  438.7 5.2 fusion.182
  446.4 5.4 fusion.179
  451.8 3.0 fusion.180
  456.5 5.2 fusion.182
  464.2 5.4 fusion.179
  469.6 3.0 fusion.180
  474.3 5.2 fusion.182
  480.6 6.0 copy.123
  486.5 4.7 reshape.332
  491.4 6.0 copy.122
  497.4 4.7 reshape.330
  504.2 64.3 %reduce-scatter.24.cloned.1.call-done = bf16[128,128]{1,0:T(8,128)(2,1)} async-done(((bf16[4096,128]{1,0:T(8,128)(2,1)}), bf16[128,128]{1,0:T(8,128)(2,1)}) %reduce-scatter.24.cloned.1.call-update) | async-done | bytes 32784
  569.4 80.0 %reduce-scatter.22.cloned.1.call-done = bf16[128,128]{1,0:T(8,128)(2,1)} async-done(((bf16[4096,128]{1,0:T(8,128)(2,1)}), bf16[128,128]{1,0:T(8,128)(2,1)}) %reduce-scatter.22.cloned.1.call-update) | async-done | bytes 32784
  652.7 7.2 convolution_convert_fusion.2
  659.9 7.2 convolution_convert_fusion.1
  668.1 4.7 convolution_convert_fusion
  672.9 5.5 reduce-scatter.14.cloned.1.call-done
  678.5 32.6 %reduce-scatter.12.cloned.1.call-done = bf16[224,1152]{1,0:T(8,128)(2,1)} async-done(((bf16[896,1152]{1,0:T(8,128)(2,1)}), bf16[224,1152]{1,0:T(8,128)(2,1)}) %reduce-scatter.12.cloned.1.call-update) | async-done | bytes 516112 | tf_op jit(solution)/shard_map/reduce_scatter | solution.py:264
  711.0 85.5 %reduce-scatter.16.cloned.1.call-done = bf16[224,4864]{1,0:T(8,128)(2,1)} async-done(((bf16[896,4864]{1,0:T(8,128)(2,1)}), bf16[224,4864]{1,0:T(8,128)(2,1)}) %reduce-scatter.16.cloned.1.call-update) | async-done | bytes 2179088 | tf_op jit(solution)/shard_map/reduce_scatter | solution.py:279
  796.5 85.2 %reduce-scatter.18.cloned.1.call-done = bf16[224,4864]{1,0:T(8,128)(2,1)} async-done(((bf16[896,4864]{1,0:T(8,128)(2,1)}), bf16[224,4864]{1,0:T(8,128)(2,1)}) %reduce-scatter.18.cloned.1.call-update) | async-done | bytes 2179088 | tf_op jit(solution)/shard_map/reduce_scatter | solution.py:282
  881.8 85.5 %reduce-scatter.20.cloned.1.call-done = bf16[1216,896]{1,0:T(8,128)(2,1)} async-done(((bf16[4864,896]{1,0:T(8,128)(2,1)}), bf16[1216,896]{1,0:T(8,128)(2,1)}) %reduce-scatter.20.cloned.1.call-update) | async-done | bytes 2179088 | tf_op jit(solution)/shard_map/reduce_scatter | solution.py:285
  969.4 5.8 fusion.65
  976.2 7.0 all-reduce.13
  983.6 65.2 %all-reduce.11 = (bf16[224]{0:T(256)(128)(2,1)S(1)}, bf16[256]{0:T(256)(128)(2,1)S(1)}, bf16[32]{0:T(256)(128)(2,1)S(1)}, bf16[224]{0:T(256)(128)(2,1)S(1)}) all-reduce(bf16[224]{0:T(256)(128)(2,1)S(1)} %dynamic-slice.4, bf16[256]{0:T(256)(128)(2,1)S(1)} %dynamic-slice.6, ...), channel_id=1, replica_groups=mesh['dp'=4,'ctx'=32] {'ctx'}, use_global_device_ids=true, to_apply=%region_18.19 | all-reduce | flops 736 | bytes 2944 | tf_op jit(solution)/shard_map/psum | solution.py:290
  1051.8 38.9 %all-reduce.17.cloned.1.call-done = (bf16[224,1152]{1,0:T(8,128)(2,1)}, bf16[224,896]{1,0:T(8,128)(2,1)}, bf16[224,4864]{1,0:T(8,128)(2,1)}, bf16[224,4864]{1,0:T(8,128)(2,1)}, bf16[1216,896]{1,0:T(8,128)(2,1)}) async-done(((bf16[224,1152]{1,0:T(8,128)(2,1)}, bf16[224,896]{1,0:T(8,128)(2,1)}, bf16[224,4864]{1,0:T(8,128)(2,1)}, bf16[224,4864]{1,0:T(8,128)(2,1)}, bf16[1216,896]{1,0:T(8,128)(2,1)}), ...) | async-done | bytes 7454736 | tf_op jit(solution)/shard_map/psum | solution.py:291
  1090.7 2.2 convert_element_type.191
  1095.0 2.3 convert_element_type.200
  1097.4 2.3 convert_element_type.202
  1099.9 2.3 convert_element_type.204
  (269 shorter events, 55.1 us)
Async XLA Ops:
  7.2 36.4 %all-gather.7.cloned.1.call-start = ((), (), s32[]{:S(2)}) async-start(), calls=%async_computation.8 | async-start | bytes 2580480 | tf_op jit(solution)/shard_map/all_gather | solution.py:82
  7.9 108.0 %all-gather.9.cloned.1.call-start = ((), (), s32[]{:S(2)}) async-start(), calls=%async_computation.9 | async-start | bytes 1081344 | tf_op jit(solution)/shard_map/all_gather | solution.py:109
  23.6 24.7 %copy-start.29 = (f32[128]{0:T(128)}, f32[128]{0:T(128)S(1)}, u32[]{:S(2)}) copy-start(f32[128]{0:T(128)S(1)} %fusion.73) | copy-start | bytes 1540
  45.8 3.2 copy-start.28
  45.8 3.5 copy-start.31
  46.5 95.6 %all-gather.11.cloned.1.call-start = ((), (), s32[]{:S(2)}) async-start(), calls=%async_computation.10 | async-start | bytes 2007040 | tf_op jit(solution)/shard_map/all_gather | solution.py:84
  47.2 162.3 %all-gather.13.cloned.1.call-start = ((), (), s32[]{:S(2)}) async-start(), calls=%async_computation.11 | async-start | bytes 10895360 | tf_op jit(solution)/shard_map/all_gather | solution.py:158
  47.8 250.1 %all-gather.15.cloned.1.call-start = ((), (), s32[]{:S(2)}) async-start(), calls=%async_computation.12 | async-start | bytes 10895360 | tf_op jit(solution)/shard_map/all_gather | solution.py:159
  48.4 337.9 %all-gather.17.cloned.1.call-start = ((), (), s32[]{:S(2)}) async-start(), calls=%async_computation.13 | async-start | bytes 10895360 | tf_op jit(solution)/shard_map/all_gather | solution.py:160
  51.2 25.2 %all-to-all-start = ((bf16[32,128,128]{1,2,0:T(8,128)(2,1)}), bf16[32,128,128]{1,2,0:T(8,128)(2,1)S(1)}, u32[]{:S(2)}, u32[]{:S(2)}) async-start(bf16[32,128,128]{1,2,0:T(8,128)(2,1)} %stack.3), calls=%async_computation | async-start | bytes 2097152 | tf_op jit(solution)/shard_map/all_to_all | solution.py:107
  58.9 509.6 %reduce-scatter.24.cloned.1.call-start = ((), (), s32[]{:S(2)}) async-start(), calls=%async_computation.20 | async-start | bytes 1081344
  126.8 15.3 %copy-start.9 = (bf16[128,896]{1,0:T(8,128)(2,1)S(1)}, bf16[128,896]{1,0:T(8,128)(2,1)}, u32[]{:S(2)}) copy-start(bf16[128,896]{1,0:T(8,128)(2,1)} %param.18) | copy-start | bytes 688132
  142.0 2.3 copy-start.19
  142.0 73.9 %copy-start.17 = (bf16[128,2,7,64]{0,3,2,1:T(8,128)(2,1)}, bf16[128,2,7,64]{0,3,2,1:T(8,128)(2,1)S(1)}, u32[]{:S(2)}) copy-start(bf16[128,2,7,64]{0,3,2,1:T(8,128)(2,1)S(1)} %convert_element_type.172) | copy-start | bytes 688132
  393.8 7.2 copy-start.12
  393.8 7.2 copy-start.11
  393.8 7.2 copy-start.2
  393.8 7.2 copy-start.4
  401.1 2.9 copy-start.24
  401.1 3.9 copy-start.8
  409.4 1.4 copy-start.26
  410.6 5.7 copy-start.1
  416.2 3.1 copy-start
  416.2 3.4 copy-start.20
  416.2 4.7 copy-start.22
  416.2 4.7 copy-start.27
  420.9 5.3 copy-start.21
  427.2 1.4 copy-start.26
  428.4 5.7 copy-start.1
  434.0 3.1 copy-start
  434.0 3.4 copy-start.20
  434.0 4.7 copy-start.22
  434.0 4.7 copy-start.27
  438.7 5.3 copy-start.21
  445.0 1.4 copy-start.26
  446.1 5.7 copy-start.1
  451.8 3.1 copy-start
  451.8 3.4 copy-start.20
  451.8 4.7 copy-start.22
  451.8 4.7 copy-start.27
  456.5 5.3 copy-start.21
  462.8 1.4 copy-start.26
  463.9 5.7 copy-start.1
  469.6 3.1 copy-start
  469.6 3.4 copy-start.20
  469.6 4.7 copy-start.22
  469.6 4.7 copy-start.27
  474.3 5.3 copy-start.21
  491.3 158.1 %reduce-scatter.22.cloned.1.call-start = ((), (), s32[]{:S(2)}) async-start(), calls=%async_computation.19 | async-start | bytes 1081344
  491.3 10.9 copy-start.7
  491.4 10.9 copy-start.18
  502.1 148.1 %copy-start.10 = (bf16[128,896]{1,0:T(8,128)(2,1)S(1)}, bf16[128,896]{1,0:T(8,128)(2,1)}, u32[]{:S(2)}) copy-start(bf16[128,896]{1,0:T(8,128)(2,1)} %param.18) | copy-start | bytes 688132
  502.2 176.3 %reduce-scatter.14.cloned.1.call-start = ((), (), s32[]{:S(2)}) async-start(), calls=%async_computation.15 | async-start | bytes 2007040 | tf_op jit(solution)/shard_map/reduce_scatter | solution.py:273
  504.0 207.0 %reduce-scatter.12.cloned.1.call-start = ((), (), s32[]{:S(2)}) async-start(), calls=%async_computation.14 | async-start | bytes 2580480 | tf_op jit(solution)/shard_map/reduce_scatter | solution.py:264
  652.4 144.1 %reduce-scatter.16.cloned.1.call-start = ((), (), s32[]{:S(2)}) async-start(), calls=%async_computation.16 | async-start | bytes 10895360 | tf_op jit(solution)/shard_map/reduce_scatter | solution.py:279
  659.9 221.9 %reduce-scatter.18.cloned.1.call-start = ((), (), s32[]{:S(2)}) async-start(), calls=%async_computation.17 | async-start | bytes 10895360 | tf_op jit(solution)/shard_map/reduce_scatter | solution.py:282
  667.2 300.1 %reduce-scatter.20.cloned.1.call-start = ((), (), s32[]{:S(2)}) async-start(), calls=%async_computation.18 | async-start | bytes 10895360 | tf_op jit(solution)/shard_map/reduce_scatter | solution.py:285
  672.9 417.9 %all-reduce.17.cloned.1.call-start = ((), (), s32[]{:S(2)}) async-start(), calls=%async_computation.21 | async-start | bytes 14909440 | tf_op jit(solution)/shard_map/psum | solution.py:291
  967.3 2.0 copy-start.5
  969.3 6.0 copy-start.16
  975.1 75.8 %copy-start.30 = (f32[128]{0:T(128)S(1)}, f32[128]{0:T(128)}, u32[]{:S(2)}) copy-start(f32[128]{0:T(128)} %copy-done.29) | copy-start | bytes 1540
  1090.7 4.3 copy-start.15
  1092.9 4.4 copy-start.14
  1097.4 2.5 copy-start.13
  (7 other events, 6.6 us)
Sparse Core Ops, SparseCore 0:
  9.7 33.8 all-gather.6
  46.6 48.2 all-gather.8
  96.6 25.5 all-gather.10
  123.7 85.8 all-gather.12
  211.0 86.8 all-gather.14
  299.4 86.8 all-gather.16
  491.4 77.0 reduce-scatter.23
  572.4 76.9 reduce-scatter.21
  652.4 26.0 reduce-scatter.13
  681.3 29.6 reduce-scatter.11
  713.7 82.8 reduce-scatter.15
  798.9 82.8 reduce-scatter.17
  884.4 82.8 reduce-scatter.19
  971.3 119.3 all-reduce.16
